TPU v7x, 512 devices: a whole 4x8x8 slice. The times are simulated.
512 devices in a mesh: tm: 16 (over y, core), nin: 8 (over z), nout: 4 (over x).
Axes of the slice: x: 4, y: 8, z: 8, core: 2. Of those that a mesh axis runs over, the one named last changes fastest.
Arguments:
- spikes: int32 [4096, 2048], P('tm', 'nin'), may hold values 0 or 1
- exposure: int32 [4096], P('tm'), may hold values from 1 to 8
- weights: bfloat16 [16384, 2048], P('nin', 'nout'), may hold values from -0.375 to 0.375
- direction: float32 [16384, 2048], P(('nin', 'tm'), 'nout'), may hold values from -6 to 6
- residual: float32 [16384, 2048], P(('nin', 'tm'), 'nout'), may hold values from -0.75 to 0.75
- iterate: float32 [16384, 2048], P(('nin', 'tm'), 'nout'), may hold values from -1.8 to 1.8
Outputs:
- new_iterate: float32 [16384, 2048], P(('nin', 'tm'), 'nout')
- new_residual: float32 [16384, 2048], P(('nin', 'tm'), 'nout')
- new_direction: float32 [16384, 2048], P(('nin', 'tm'), 'nout')
All inputs are finite; a program needn't handle non-finite values. No bound on the sum of `spikes` on one device may be relied on, other than what follows from the above.
Results may differ from a plain program's by a relative error of at most 0.015.
Values may be sent and summed in bfloat16 or wider, within the bound.
A program may use at most 64 MiB of HBM per device.

v0:
```python
import math
import jax
import jax.numpy as jnp
from jax import lax
from jax.sharding import PartitionSpec as P

BASES = 8
HISTORY = 128
RIDGE_WEIGHT = 0.05
NORM_EPS = 1e-06


def shifted(value, axis, steps):
    count = lax.axis_size(axis)
    initial, last = (max(0, -steps), min(count, count - steps))
    return lax.ppermute(value, axis, [(source, source + steps) for source in range(initial, last)])


def basis_table(history, bases_count):
    lag_values = jnp.arange(1, history + 1, dtype=jnp.float32)
    warped = jnp.log(lag_values + 1.0)
    log_low = math.log(2.0)
    log_high = math.log(history + 1.0)
    spacing = (log_high - log_low) / (bases_count - 1)
    centers = log_low + spacing * jnp.arange(bases_count, dtype=jnp.float32)
    phases = (warped[:, None] - centers[None, :]) * (math.pi / (2.0 * spacing))
    phases = jnp.clip(phases, -math.pi, math.pi)
    bump_values = 0.5 * (1.0 + jnp.cos(phases))
    bump_values = bump_values / jnp.sum(bump_values, axis=0, keepdims=True)
    return bump_values.astype(jnp.bfloat16)


def lag_kernel(basis_rows, span, offset):
    out_index = jnp.arange(span, dtype=jnp.int32)[:, None]
    in_index = jnp.arange(span, dtype=jnp.int32)[None, :]
    lag_index = out_index + offset - in_index
    is_valid = (lag_index >= 1) & (lag_index <= HISTORY)
    take_index = jnp.clip(lag_index - 1, 0, HISTORY - 1)
    return jnp.where(
        is_valid[None], jnp.take(basis_rows.T, take_index, axis=1), jnp.zeros((), jnp.bfloat16)
    )


def per_device(spikes, exposure, weights, direction, residual, iterate):
    block_rows = spikes.shape[0]
    neuron_cols = spikes.shape[1]
    basis_rows = basis_table(HISTORY, BASES)
    spike_low = spikes.astype(jnp.bfloat16)
    block_count = block_rows // HISTORY
    stacked = spike_low.reshape(block_count, HISTORY, neuron_cols)
    kernel_same = lag_kernel(basis_rows, HISTORY, 0)
    kernel_before = lag_kernel(basis_rows, HISTORY, HISTORY)
    current = jnp.einsum("bim,cmn->cinb", kernel_same, stacked, preferred_element_type=jnp.float32)
    tail_part = jnp.einsum(
        "bim,mn->inb", kernel_before, stacked[-1], preferred_element_type=jnp.float32
    )
    inner_part = jnp.einsum(
        "bim,cmn->cinb", kernel_before, stacked[:-1], preferred_element_type=jnp.float32
    )
    tail_terms = shifted(tail_part.astype(jnp.bfloat16), "tm", 1).astype(tail_part.dtype)
    own_terms = current + jnp.concatenate([tail_terms[None], inner_part], axis=0)
    features = own_terms.reshape(block_rows, neuron_cols * BASES).astype(jnp.bfloat16)
    direction_low = direction.astype(jnp.bfloat16)
    columns = features
    along_part = jnp.dot(
        columns,
        lax.all_gather(direction_low, "tm", axis=0, tiled=True),
        preferred_element_type=jnp.float32,
    )
    predictor_part = jnp.dot(features, weights, preferred_element_type=jnp.float32)
    tick_scale = exposure.astype(jnp.float32) / 8.0
    predictor_full, along_full = (
        lax.psum(predictor_part.astype(jnp.bfloat16), "nin").astype(jnp.float32),
        lax.psum(along_part.astype(jnp.bfloat16), "nin").astype(jnp.float32),
    )
    weighted = (tick_scale[:, None] * jnp.exp(predictor_full) * along_full).astype(jnp.bfloat16)
    columns = features
    gram = lax.psum_scatter(
        lax.dot_general(
            columns, weighted, (((0,), (0,)), ((), ())), preferred_element_type=jnp.float32
        ).astype(jnp.bfloat16),
        "tm",
        scatter_dimension=0,
        tiled=True,
    ).astype(jnp.float32)
    bin_total = block_rows * lax.axis_size("tm")
    curvature_prod = gram / bin_total + RIDGE_WEIGHT * direction
    old_norm, curvature = lax.psum(
        (jnp.sum(residual * residual, axis=0), jnp.sum(direction * curvature_prod, axis=0)),
        ("tm", "nin"),
    )
    step_size = old_norm / curvature
    new_iterate = iterate + step_size[None, :] * direction
    new_residual = residual - step_size[None, :] * curvature_prod
    new_norm = lax.psum(jnp.sum(new_residual * new_residual, axis=0), ("tm", "nin"))
    new_direction = new_residual + (new_norm / (old_norm + NORM_EPS))[None, :] * direction
    return (new_iterate, new_residual, new_direction)


def solution(mesh):
    in_specs = (
        P("tm", "nin"),
        P("tm"),
        P("nin", "nout"),
        P(("nin", "tm"), "nout"),
        P(("nin", "tm"), "nout"),
        P(("nin", "tm"), "nout"),
    )
    out_specs = (P(("nin", "tm"), "nout"), P(("nin", "tm"), "nout"), P(("nin", "tm"), "nout"))
    return jax.shard_map(
        per_device, mesh=mesh, in_specs=in_specs, out_specs=out_specs, check_vma=False
    )
```

profile of v0, /device:TPU:2, one launch (start us, length us, event | category | flops | bytes accessed | tf_op | source)
XLA Modules:
  0.0 800.1 jit_solution(18235166921538115580)
XLA Ops:
  7.2 0.0 copy-start
  7.2 0.0 all-gather.2.cloned.1.call-start
  7.2 1.8 convert_element_type.56
  9.0 0.0 all-gather.2.cloned.1.call-update
  9.0 0.0 all-reduce.4.cloned.1.call-start
  9.1 0.2 multiply_reduce_fusion.3
  9.3 0.1 divide_convert_fusion
  9.4 0.1 copy.17
  9.6 0.1 bitcast_clamp_fusion
  9.7 57.8 %gather_fusion.1 = bf16[16384,8]{1,0:T(8,128)(2,1)} fusion(bf16[8,128]{0,1:T(8,128)(2,1)S(1)} %copy.17, s32[16384]{0:T(1024)S(1)} %bitcast_clamp_fusion), kind=kCustom, calls=%fused_computation.1.clone | custom fusion | bytes 589824 | tf_op jit(solution)/shard_map/jit(_take)/gather | solution.py:40
  67.5 0.0 copy-start.5
  67.5 3.6 copy.20
  71.2 0.0 copy-done.5
  71.2 0.1 fusion.30
  71.3 1.1 fusion.1
  72.4 1.8 collective-permute-start
  74.2 57.8 %gather_fusion = bf16[16384,8]{1,0:T(8,128)(2,1)} fusion(bf16[8,128]{0,1:T(8,128)(2,1)S(1)} %copy.17, s32[16384]{0:T(1024)S(1)} %bitcast_clamp_fusion.1), kind=kCustom, calls=%fused_computation.clone | custom fusion | bytes 589824 | tf_op jit(solution)/shard_map/jit(_take)/gather | solution.py:40
  132.0 3.6 copy.18
  135.6 0.1 fusion.27
  135.7 0.3 convolution_bitcast_fusion
  136.0 0.0 collective-permute-done
  136.0 0.1 bitcast_convert_fusion
  136.1 0.4 fusion
  136.5 2.1 copy.21
  138.6 0.0 copy-done
  138.6 0.0 copy-start.2
  138.6 2.8 convolution_convert_fusion.3
  141.4 0.0 all-gather.2.cloned.1.call-done
  141.4 0.0 copy-done.2
  141.4 3.0 convolution_convert_fusion.2
  144.4 0.0 all-reduce.4.cloned.1.call-update
  144.5 0.0 reduce-scatter.2.cloned.1.call-start
  144.5 0.0 copy-done.7
  144.5 85.0 %all-reduce.4.cloned.1.call-done = (bf16[256,512]{1,0:T(8,128)(2,1)}, bf16[256,512]{1,0:T(8,128)(2,1)}) async-done(((bf16[256,512]{1,0:T(8,128)(2,1)}, bf16[256,512]{1,0:T(8,128)(2,1)}), (bf16[256,512]{1,0:T(8,128)(2,1)}, bf16[256,512]{1,0:T(8,128)(2,1)})) %all-reduce.4.cloned.1.call-update) | async-done | bytes 524304 | tf_op jit(solution)/shard_map/psum | solution.py:74
  229.5 0.0 copy-start.4
  229.5 3.2 convolution_convert_fusion
  232.8 0.0 copy-start.1
  232.8 0.0 reduce-scatter.2.cloned.1.call-update
  232.8 0.0 copy-done.4
  232.9 59.8 %reduce-scatter.2.cloned.1.call-done = bf16[128,512]{1,0:T(8,128)(2,1)} async-done(((bf16[2048,512]{1,0:T(8,128)(2,1)}), bf16[128,512]{1,0:T(8,128)(2,1)}) %reduce-scatter.2.cloned.1.call-update) | async-done | bytes 131088 | tf_op jit(solution)/shard_map/reduce_scatter | solution.py:78
  292.7 0.0 copy-done.1
  292.7 1.0 multiply_reduce_fusion.1
  293.6 250.6 %all-reduce = (f32[512]{0:T(512)S(1)}, f32[512]{0:T(512)S(1)}) all-reduce(f32[512]{0:T(512)S(1)} %multiply_reduce_fusion.2, f32[512]{0:T(512)S(1)} %multiply_reduce_fusion.1), channel_id=1, replica_groups=mesh['tm'=16,'nin'=8,'nout'=4] {'tm','nin'}, use_global_device_ids=true, to_apply=%region_1.2 | all-reduce | flops 1024 | bytes 8192 | tf_op jit(solution)/shard_map/psum | solution.py:88
  544.3 0.0 copy-done.6
  544.3 1.7 multiply_reduce_fusion
  546.0 246.8 %psum.39 = f32[512]{0:T(512)S(1)} all-reduce(f32[512]{0:T(512)S(1)} %get-tuple-element.8), channel_id=1, replica_groups=mesh['tm'=16,'nin'=8,'nout'=4] {'tm','nin'}, use_global_device_ids=true, to_apply=%region_9.11 | all-reduce | flops 512 | bytes 4096 | tf_op jit(solution)/shard_map/psum | solution.py:95
  792.8 0.8 multiply_add_fusion
  793.5 0.0 copy-done.3
  (12 shorter events, 0.1 us)
Async XLA Ops:
  7.2 131.5 %copy-start = (bf16[2048,512]{1,0:T(8,128)(2,1)S(1)}, bf16[2048,512]{1,0:T(8,128)(2,1)}, u32[]{:S(2)}) copy-start(bf16[2048,512]{1,0:T(8,128)(2,1)} %param.10) | copy-start | bytes 6291460
  7.2 134.2 %all-gather.2.cloned.1.call-start = ((), (), s32[]{:S(2)}) async-start(), calls=%async_computation.1 | async-start | bytes 2228224 | tf_op jit(solution)/shard_map/all_gather | solution.py:67
  9.0 220.5 %all-reduce.4.cloned.1.call-start = ((), (), s32[]{:S(2)}) async-start(), calls=%async_computation.3 | async-start | bytes 1048576 | tf_op jit(solution)/shard_map/psum | solution.py:74
  67.5 3.6 copy-start.5
  72.4 63.6 %collective-permute-start = (bf16[128,256,8]{1,0,2:T(8,128)(2,1)}, bf16[128,256,8]{1,0,2:T(8,128)(2,1)S(1)}, u32[]{:S(2)}, u32[]{:S(2)}) collective-permute-start(bf16[128,256,8]{1,0,2:T(8,128)(2,1)} %fusion.1), channel_id=1, source_target_pairs={{0,32},{32,64},{64,96},{96,128},{128,160},{160,192},{192,224},{224... | collective-permute-start | bytes 1572872 | tf_op jit(solution)/shard_map/ppermute | solution.py:16
  138.6 2.8 copy-start.2
  141.4 3.1 copy-start.7
  144.5 148.2 %reduce-scatter.2.cloned.1.call-start = ((), (), s32[]{:S(2)}) async-start(), calls=%async_computation.2 | async-start | bytes 2228224 | tf_op jit(solution)/shard_map/reduce_scatter | solution.py:78
  229.5 3.3 copy-start.4
  232.8 59.9 %copy-start.1 = (f32[128,512]{1,0:T(8,128)S(1)}, f32[128,512]{1,0:T(8,128)}, u32[]{:S(2)}) copy-start(f32[128,512]{1,0:T(8,128)} %param.11) | copy-start | bytes 786436
  232.8 311.5 %copy-start.6 = (f32[128,512]{1,0:T(8,128)S(1)}, f32[128,512]{1,0:T(8,128)}, u32[]{:S(2)}) copy-start(f32[128,512]{1,0:T(8,128)} %param.13) | copy-start | bytes 786436
  546.0 247.6 %copy-start.3 = (f32[128,512]{1,0:T(8,128)}, f32[128,512]{1,0:T(8,128)S(1)}, u32[]{:S(2)}) copy-start(f32[128,512]{1,0:T(8,128)S(1)} %get-tuple-element.9) | copy-start | bytes 786436
Sparse Core Ops, SparseCore 0:
  10.7 46.5 all-gather.1
  144.6 84.9 all-reduce.3
  232.9 59.6 reduce-scatter.1
where the time goes:
time: 800 us
  blocking collectives  497 us (62%)
  waiting for transfers between devices  145 us (18%)
  local copies, waits for them, and re-layouts  125 us (16%)
  between operations  13.9 us (2%)
  matrix products  10.8 us (1%)
    psum x1, blocking collectives, per_device(): lax.psum((jnp.sum(residual * residual, axis=0), jnp.sum(direction * curva...  251 us
    psum x1, blocking collectives, per_device(): lax.psum(jnp.sum(new_residual * new_residual, axis=0), ('tm', 'nin'))  247 us
    gather x4, local copies, waits for them, and re-layouts, lag_kernel(): jnp.take(basis_rows.T, take_index, axis=1)  123 us
    psum x1, waiting for transfers between devices, per_device(): lax.psum(along_part.astype(jnp.bfloat16), 'nin').astype(jnp.float32)  85 us
    reduce_scatter x1, waiting for transfers between devices, per_device(): lax.psum_scatter(lax.dot_general(columns, weighted, (((0,), (0,)), ((), (...  59.8 us
  transfers between devices with their start and end apart: 4, of which 2 were waited for; matrix products, arithmetic and copies ran while one was open for 16% of the time, Pallas kernels for 0%

commit v1 on v0

--- a/solution.py
+++ b/solution.py
@@ -92,7 +92,9 @@
     step_size = old_norm / curvature
     new_iterate = iterate + step_size[None, :] * direction
     new_residual = residual - step_size[None, :] * curvature_prod
-    new_norm = lax.psum(jnp.sum(new_residual * new_residual, axis=0), ("tm", "nin"))
+    new_norm = jnp.sum(
+        lax.all_gather(jnp.sum(new_residual * new_residual, axis=0), ("tm", "nin")), axis=0
+    )
     new_direction = new_residual + (new_norm / (old_norm + NORM_EPS))[None, :] * direction
     return (new_iterate, new_residual, new_direction)
 

time: 800 us -> 643 us (0.80)
  the two profiles are of different devices: /device:TPU:2 before, /device:TPU:27 now
where the time goes in v1:
time: 643 us
  blocking collectives  340 us (53%)
  waiting for transfers between devices  142 us (22%)
  local copies, waits for them, and re-layouts  125 us (19%)
  between operations  13.9 us (2%)
  matrix products  10.8 us (2%)
    psum x1, blocking collectives, per_device(): lax.psum((jnp.sum(residual * residual, axis=0), jnp.sum(direction * curva...  236 us
    gather x4, local copies, waits for them, and re-layouts, lag_kernel(): jnp.take(basis_rows.T, take_index, axis=1)  123 us
    all_gather x1, blocking collectives, per_device(): lax.all_gather(jnp.sum(new_residual * new_residual, axis=0), ('tm', 'nin'))  104 us
    psum x1, waiting for transfers between devices, per_device(): lax.psum(along_part.astype(jnp.bfloat16), 'nin').astype(jnp.float32)  77.2 us
    reduce_scatter x1, waiting for transfers between devices, per_device(): lax.psum_scatter(lax.dot_general(columns, weighted, (((0,), (0,)), ((), (...  64.4 us
  transfers between devices with their start and end apart: 4, of which 2 were waited for; matrix products, arithmetic and copies ran while one was open for 20% of the time, Pallas kernels for 0%

profile of v1, /device:TPU:27, one launch (start us, length us, event | category | flops | bytes accessed | tf_op | source)
XLA Modules:
  0.0 642.5 jit_solution(2034350802071964556)
XLA Ops:
  7.2 0.0 copy-start
  7.2 0.0 all-gather.4.cloned.1.call-start
  7.2 1.8 convert_element_type.56
  9.0 0.0 all-gather.4.cloned.1.call-update
  9.0 0.0 all-reduce.4.cloned.1.call-start
  9.1 0.2 multiply_reduce_fusion.3
  9.3 0.1 divide_convert_fusion
  9.4 0.1 copy.20
  9.6 0.1 bitcast_clamp_fusion
  9.7 57.8 %gather_fusion.1 = bf16[16384,8]{1,0:T(8,128)(2,1)} fusion(bf16[8,128]{0,1:T(8,128)(2,1)S(1)} %copy.20, s32[16384]{0:T(1024)S(1)} %bitcast_clamp_fusion), kind=kCustom, calls=%fused_computation.1.clone | custom fusion | bytes 589824 | tf_op jit(solution)/shard_map/jit(_take)/gather | solution.py:40
  67.5 0.0 copy-start.5
  67.5 3.6 copy.23
  71.2 0.0 copy-done.5
  71.2 0.1 fusion.30
  71.3 1.1 fusion.1
  72.4 5.0 collective-permute-start
  77.4 57.8 %gather_fusion = bf16[16384,8]{1,0:T(8,128)(2,1)} fusion(bf16[8,128]{0,1:T(8,128)(2,1)S(1)} %copy.20, s32[16384]{0:T(1024)S(1)} %bitcast_clamp_fusion.1), kind=kCustom, calls=%fused_computation.clone | custom fusion | bytes 589824 | tf_op jit(solution)/shard_map/jit(_take)/gather | solution.py:40
  135.2 3.6 copy.21
  138.8 0.1 fusion.27
  138.9 0.3 convolution_bitcast_fusion
  139.2 0.0 collective-permute-done
  139.2 0.1 bitcast_convert_fusion
  139.3 0.4 fusion
  139.7 2.1 copy.24
  141.8 0.0 copy-done
  141.8 2.8 convolution_convert_fusion.3
  144.6 0.0 copy-start.7
  144.6 0.0 all-gather.4.cloned.1.call-done
  144.6 0.0 copy-done.2
  144.6 3.1 convolution_convert_fusion.2
  147.6 0.0 all-reduce.4.cloned.1.call-update
  147.7 0.0 reduce-scatter.2.cloned.1.call-start
  147.7 0.0 copy-done.7
  147.7 77.2 %all-reduce.4.cloned.1.call-done = (bf16[256,512]{1,0:T(8,128)(2,1)}, bf16[256,512]{1,0:T(8,128)(2,1)}) async-done(((bf16[256,512]{1,0:T(8,128)(2,1)}, bf16[256,512]{1,0:T(8,128)(2,1)}), (bf16[256,512]{1,0:T(8,128)(2,1)}, bf16[256,512]{1,0:T(8,128)(2,1)})) %all-reduce.4.cloned.1.call-update) | async-done | bytes 524304 | tf_op jit(solution)/shard_map/psum | solution.py:74
  224.9 0.0 copy-start.4
  224.9 3.2 convolution_convert_fusion
  228.2 0.0 reduce-scatter.2.cloned.1.call-update
  228.2 0.0 copy-done.4
  228.2 64.4 %reduce-scatter.2.cloned.1.call-done = bf16[128,512]{1,0:T(8,128)(2,1)} async-done(((bf16[2048,512]{1,0:T(8,128)(2,1)}), bf16[128,512]{1,0:T(8,128)(2,1)}) %reduce-scatter.2.cloned.1.call-update) | async-done | bytes 131088 | tf_op jit(solution)/shard_map/reduce_scatter | solution.py:78
  292.7 0.0 copy-done.1
  292.7 1.0 multiply_reduce_fusion.1
  293.6 235.6 %all-reduce = (f32[512]{0:T(512)S(1)}, f32[512]{0:T(512)S(1)}) all-reduce(f32[512]{0:T(512)S(1)} %multiply_reduce_fusion.2, f32[512]{0:T(512)S(1)} %multiply_reduce_fusion.1), channel_id=1, replica_groups=mesh['tm'=16,'nin'=8,'nout'=4] {'tm','nin'}, use_global_device_ids=true, to_apply=%region_1.2 | all-reduce | flops 1024 | bytes 8192 | tf_op jit(solution)/shard_map/psum | solution.py:88
  529.3 0.0 copy-done.6
  529.3 1.7 multiply_reduce_fusion
  531.0 104.1 %all-gather.1 = f32[128,1,512]{2,1,0:T(1,128)S(1)} all-gather(f32[1,1,512]{2,1,0:T(1,128)S(1)} %bitcast.63), channel_id=2, replica_groups=mesh['tm'=16,'nin'=8,'nout'=4] {'tm','nin'}, dimensions={0}, use_global_device_ids=true | all-gather | bytes 264192 | tf_op jit(solution)/shard_map/all_gather | solution.py:96
  635.0 0.2 reduce_sum.49
  635.3 0.8 multiply_add_fusion
  636.0 0.0 copy-done.3
  (13 shorter events, 0.1 us)
Async XLA Ops:
  7.2 134.7 %copy-start = (bf16[2048,512]{1,0:T(8,128)(2,1)S(1)}, bf16[2048,512]{1,0:T(8,128)(2,1)}, u32[]{:S(2)}) copy-start(bf16[2048,512]{1,0:T(8,128)(2,1)} %param.10) | copy-start | bytes 6291460
  7.2 137.4 %all-gather.4.cloned.1.call-start = ((), (), s32[]{:S(2)}) async-start(), calls=%async_computation.1 | async-start | bytes 2228224 | tf_op jit(solution)/shard_map/all_gather | solution.py:67
  9.0 215.9 %all-reduce.4.cloned.1.call-start = ((), (), s32[]{:S(2)}) async-start(), calls=%async_computation.3 | async-start | bytes 1048576 | tf_op jit(solution)/shard_map/psum | solution.py:74
  67.5 3.6 copy-start.5
  72.4 66.8 %collective-permute-start = (bf16[128,256,8]{1,0,2:T(8,128)(2,1)}, bf16[128,256,8]{1,0,2:T(8,128)(2,1)S(1)}, u32[]{:S(2)}, u32[]{:S(2)}) collective-permute-start(bf16[128,256,8]{1,0,2:T(8,128)(2,1)} %fusion.1), channel_id=1, source_target_pairs={{0,32},{32,64},{64,96},{96,128},{128,160},{160,192},{192,224},{224... | collective-permute-start | bytes 1572872 | tf_op jit(solution)/shard_map/ppermute | solution.py:16
  141.8 2.8 copy-start.2
  144.6 3.1 copy-start.7
  147.7 145.0 %reduce-scatter.2.cloned.1.call-start = ((), (), s32[]{:S(2)}) async-start(), calls=%async_computation.2 | async-start | bytes 2228224 | tf_op jit(solution)/shard_map/reduce_scatter | solution.py:78
  224.9 3.3 copy-start.4
  228.2 64.5 %copy-start.1 = (f32[128,512]{1,0:T(8,128)S(1)}, f32[128,512]{1,0:T(8,128)}, u32[]{:S(2)}) copy-start(f32[128,512]{1,0:T(8,128)} %param.11) | copy-start | bytes 786436
  228.2 301.1 %copy-start.6 = (f32[128,512]{1,0:T(8,128)S(1)}, f32[128,512]{1,0:T(8,128)}, u32[]{:S(2)}) copy-start(f32[128,512]{1,0:T(8,128)} %param.13) | copy-start | bytes 786436
  531.0 105.1 %copy-start.3 = (f32[128,512]{1,0:T(8,128)}, f32[128,512]{1,0:T(8,128)S(1)}, u32[]{:S(2)}) copy-start(f32[128,512]{1,0:T(8,128)S(1)} %get-tuple-element.9) | copy-start | bytes 786436
Sparse Core Ops, SparseCore 0:
  10.7 46.3 all-gather.3
  147.8 77.0 all-reduce.3
  228.3 64.3 reduce-scatter.1
